TPU v7x, 32 devices: a whole 2x2x4 slice. The times are simulated.
32 devices in a mesh: groups: 2 (over y), space: 4 (over z), phase: 4 (over x, core).
Axes of the slice: x: 2, y: 2, z: 4, core: 2. Of those that a mesh axis runs over, the one named last changes fastest.
Arguments:
- intensity: float32 [16, 131072], P('phase', ('groups', 'space')), parts along dimension 1, may hold values from -6 to 6
- image_grad: bfloat16 [3, 16, 131072], P(None, 'phase', ('groups', 'space')), parts along dimension 2, may hold values from -6 to 6
- owner: int32 [131072, 1], P(('groups', 'space')), parts along dimension 0, may hold values from 0 to 3; in each aligned block of 16384 rows (0 to 16383, 16384 to 32767, ...) at most 8192 rows name the same one
- coord_xy: int32 [2, 131072], P(None, ('groups', 'space')), parts along dimension 1, may hold values from 0 to 463
- coord_z: int32 [131072], P(('groups', 'space')), parts along dimension 0, may hold values from 0 to 127
Outputs:
- control_grad: float32 [6, 16, 32, 1024], P('groups', 'phase', 'space'), parts along dimension 0
There are 2 independent parts, one for each index of `groups`. A program takes and returns all parts, laid end to end along the dimension named above; each array names one. Nothing has to cross between parts.
Inputs may be any that keep to these rules, and one draw needn't show every extreme that they name: Of the samples of one device, at most 8192 name the same owner, and some device has exactly 8192 samples for some owner.
All inputs are finite; a program needn't handle non-finite values.
Results may differ from a plain program's by a relative error of at most 0.0041.
Values sent between devices are 32-bit elements; how exact they have to be, the bound alone decides.
A program may use at most 64 MiB of HBM per device.

v0:
```python
import jax
import jax.numpy as jnp
from jax import lax
from jax.sharding import PartitionSpec as P

GX = 32
SPC = 16
GZ_DEV = 8


def shifted(block, axis, distance):
    devices = range(lax.axis_size(axis))
    route = [(i - distance, i) for i in devices if i - distance in devices]
    return lax.ppermute(block, axis, route)


def spline_values(offset):
    square = offset * offset
    cube = square * offset
    remain = 1.0 - offset
    return (
        remain * remain * remain / 6.0,
        (3.0 * cube - 6.0 * square + 4.0) / 6.0,
        (-3.0 * cube + 3.0 * square + 3.0 * offset + 1.0) / 6.0,
        cube / 6.0,
    )


def spread(position, extent):
    corner = jnp.floor(position)
    offset = position - corner
    values = spline_values(offset)
    distance = jnp.arange(extent, dtype=jnp.int32)[None, :] - corner.astype(jnp.int32)[:, None]
    weights = jnp.zeros((position.shape[0], extent), jnp.float32)
    for which, value in enumerate(values):
        weights = jnp.where(distance == which, value[:, None], weights)
    return weights


def block_grad(forces, positions):
    along_x = spread(positions[0], GX)
    along_y = spread(positions[1], GX)
    along_z = spread(positions[2], GZ_DEV + 3)
    plane = (along_x[:, :, None] * along_y[:, None, :]).reshape(-1, GX * GX).astype(jnp.bfloat16)
    lifted = (
        (forces[:, None, :] * along_z.T[None, :, :])
        .reshape(-1, forces.shape[1])
        .astype(jnp.bfloat16)
    )
    return jnp.dot(lifted, plane, preferred_element_type=jnp.float32)


def local(intensity, image_grad, owner, coord_xy, coord_z):
    ph_dev, s_dev = intensity.shape
    n_space = lax.axis_size("space")
    capacity = 2 * s_dev // n_space
    force_rows = 3 * ph_dev
    panels = lax.all_gather(intensity, "phase", axis=0, tiled=True)
    phase_mean = jnp.mean(panels, axis=0)
    centered_all = panels - phase_mean
    phase_var = jnp.mean(centered_all * centered_all, axis=0)
    deviation = 2.0 * (intensity - phase_mean) / jnp.sqrt(phase_var + 1.0)
    forces = (deviation[None] * image_grad.astype(jnp.float32)).reshape(force_rows, s_dev)
    positions = jnp.stack(
        [
            coord_xy[0].astype(jnp.float32) / SPC,
            coord_xy[1].astype(jnp.float32) / SPC,
            coord_z.astype(jnp.float32) / SPC,
        ],
        axis=0,
    )
    payload = jnp.concatenate([forces, positions], axis=0)
    target = owner[:, 0]
    matches = (target[:, None] == jnp.arange(n_space, dtype=jnp.int32)[None, :]).astype(jnp.int32)
    order_in = jnp.cumsum(matches, axis=0) - 1
    slot_index = jnp.sum(order_in * matches, axis=1)
    empty = jnp.concatenate(
        [
            jnp.zeros((n_space, force_rows, capacity), jnp.float32),
            -jnp.ones((n_space, 3, capacity), jnp.float32),
        ],
        axis=1,
    )
    buckets = empty.at[target, :, slot_index].set(payload.T)
    received = lax.all_to_all(buckets, "space", split_axis=0, concat_axis=0, tiled=True)
    start_grid = jnp.zeros((force_rows * (GZ_DEV + 3), GX * GX), jnp.float32)
    used_rows = jnp.sum((received[:, force_rows, :] >= 0.0).astype(jnp.int32), axis=1)
    step_rows = min(512, capacity)

    def add_bucket(bucket, running_grid):
        bucket_rows = received[bucket]

        def add_block(block_id, inner_grid):
            section = lax.dynamic_slice_in_dim(bucket_rows, block_id * step_rows, step_rows, 1)
            return inner_grid + block_grad(section[:force_rows], section[force_rows:])

        block_total = (used_rows[bucket] + step_rows - 1) // step_rows
        return lax.fori_loop(0, block_total, add_block, running_grid)

    local_grid = lax.fori_loop(0, n_space, add_bucket, start_grid)
    planes = local_grid.reshape(force_rows, GZ_DEV + 3, GX * GX)
    owned_planes = planes[:, :GZ_DEV]
    ghost_rows = planes[:, GZ_DEV:]
    incoming = shifted(ghost_rows, "space", 1)
    owned_planes = owned_planes.at[:, :3].add(incoming)
    return owned_planes.reshape(3, ph_dev, GZ_DEV, GX * GX)


def solution(mesh):
    return jax.shard_map(
        local,
        mesh=mesh,
        in_specs=(
            P("phase", ("groups", "space")),
            P(None, "phase", ("groups", "space")),
            P(("groups", "space"), None),
            P(None, ("groups", "space")),
            P(("groups", "space")),
        ),
        out_specs=P("groups", "phase", "space", None),
        check_vma=False,
    )
```

profile of v0, /device:TPU:20, one launch (start us, length us, event | category | flops | bytes accessed | tf_op | source)
XLA Modules:
  0.0 254.9 jit_solution(12700552280051949923)
XLA Ops:
  6.5 0.7 all-gather.3.cloned.1.call-update
  7.3 0.9 copy.18
  8.5 0.3 reduce-window.9
  9.0 1.2 fusion.40
  10.2 1.0 compare_select_fusion
  11.1 1.1 convert_multiply_fusion.3
  12.3 0.9 multiply_reduce_fusion.1
  13.2 1.0 and_reduce_fusion
  14.2 0.8 convert_multiply_fusion.1
  15.0 11.7 %all-gather.3.cloned.1.call-done = f32[4,4,16384]{2,1,0:T(4,128)} async-done(((f32[1,4,16384]{2,1,0:T(4,128)}), f32[4,4,16384]{2,1,0:T(4,128)}) %all-gather.3.cloned.1.call-update) | async-done | bytes 1048592 | tf_op jit(solution)/shard_map/all_gather | solution.py:58
  26.7 1.5 reduce_sum.40
  28.2 1.6 reshape.506
  30.3 0.3 reshape.492
  30.9 4.7 %copy.20 = f32[16384,15]{1,0:T(8,128)} copy(f32[16384,15]{0,1:T(8,128)S(1)} %maximum_bitcast_fusion) | data formatting | bytes 1966080 | tf_op jit(solution)/shard_map/transpose | solution.py:84
  35.5 6.0 %broadcast.556 = f32[15,32768]{0,1:T(8,128)} broadcast(f32[15]{0:T(128)S(1)} %concatenate.13), dimensions={0} | broadcast | bytes 1966140
  41.5 52.1 %scatter_fusion = f32[15,32768]{0,1:T(8,128)} fusion(f32[15,32768]{0,1:T(8,128)} %broadcast.556, s32[16384]{0:T(1024)S(1)} %broadcast_select_fusion, f32[16384,15]{1,0:T(8,128)} %copy.20), kind=kCustom, calls=%fused_computation | custom fusion | bytes 3014656
  93.6 10.8 %copy.21 = f32[15,4,8192]{2,0,1:T(8,128)} copy(f32[15,4,8192]{0,2,1:T(8,128)} %bitcast.50) | data formatting | bytes 3932160
  104.4 5.1 %all-to-all-start = ((f32[4,15,8192]{2,1,0:T(8,128)}), f32[4,15,8192]{2,1,0:T(8,128)}, u32[]{:S(2)}, u32[]{:S(2)}) async-start(f32[4,15,8192]{2,1,0:T(8,128)} %bitcast.15), calls=%async_computation | async-start | bytes 4194304 | tf_op jit(solution)/shard_map/all_to_all | solution.py:85
  109.5 45.4 %all-to-all-done = f32[4,15,8192]{2,1,0:T(8,128)} async-done(((f32[4,15,8192]{2,1,0:T(8,128)}), f32[4,15,8192]{2,1,0:T(8,128)}, u32[]{:S(2)}, u32[]{:S(2)}) %all-to-all-start) | async-done | bytes 1966112 | tf_op jit(solution)/shard_map/all_to_all | solution.py:85
  154.9 1.6 fusion.42
  156.5 39.9 %while.54 = (s32[]{:T(128)}, f32[132,1024]{1,0:T(8,128)S(1)}, s32[4]{0:T(128)S(1)}, f32[4,15,8192]{2,1,0:T(8,128)}, s32[]{:T(128)}, /*index=5*/s32[]{:T(128)}, s...) while((s32[]{:T(128)}, f32[132,1024]{1,0:T(8,128)S(1)}, ...), condition=%wide.region_10.11_spmd, body=%wide.region_7.10_spmd.sunk | while | flops 140110352 | bytes 5163650 | solution.py:100
  156.5 0.6 dynamic_slice.35
  157.8 1.1 dynamic-slice_bitcast_fusion.2
  158.8 9.1 %while.55 = (s32[]{:T(128)}, f32[132,1024]{1,0:T(8,128)S(1)}, s32[]{:T(128)}, f32[15,8192]{1,0:T(8,128)S(1)}, s32[]{:T(128)}, /*index=5*/s32[]{:T(128)}, s32[]{}, s32[]{:T(128)}, s32[]{:T(128)}, s32[]{}, /*index=10*/s32[]{}) while((s32[]{:T(128)}, f32[132,1024]{1,0:T(8,128)S(1)}, s32[]{:T(128)}, f32[15,8192]{1,0:T(8,128)S(1)}, s32[]{:T(128)}, ...), condition=%wide.region_9.9_spmd, body=%wide.region_8.8_spmd.sunk | while | flops 140110336 | bytes 4180179 | solution.py:98
  159.5 0.5 convolution_add_fusion.2
  160.6 0.5 convolution_add_fusion.2
  161.7 0.5 convolution_add_fusion.2
  162.9 0.5 convolution_add_fusion.2
  164.0 0.5 convolution_add_fusion.2
  165.1 0.5 convolution_add_fusion.2
  166.3 0.5 convolution_add_fusion.2
  167.4 0.5 convolution_add_fusion.2
  167.9 0.6 dynamic_slice.35
  169.2 1.1 dynamic-slice_bitcast_fusion.2
  170.2 6.8 %while.55 = (s32[]{:T(128)}, f32[132,1024]{1,0:T(8,128)S(1)}, s32[]{:T(128)}, f32[15,8192]{1,0:T(8,128)S(1)}, s32[]{:T(128)}, /*index=5*/s32[]{:T(128)}, s32[]{}, s32[]{:T(128)}, s32[]{:T(128)}, s32[]{}, /*index=10*/s32[]{}) while((s32[]{:T(128)}, f32[132,1024]{1,0:T(8,128)S(1)}, s32[]{:T(128)}, f32[15,8192]{1,0:T(8,128)S(1)}, s32[]{:T(128)}, ...), condition=%wide.region_9.9_spmd, body=%wide.region_8.8_spmd.sunk | while | flops 140110336 | bytes 4180179 | solution.py:98
  170.9 0.5 convolution_add_fusion.2
  172.0 0.5 convolution_add_fusion.2
  173.1 0.5 convolution_add_fusion.2
  174.3 0.5 convolution_add_fusion.2
  175.4 0.5 convolution_add_fusion.2
  176.5 0.5 convolution_add_fusion.2
  177.1 0.6 dynamic_slice.35
  178.3 1.1 dynamic-slice_bitcast_fusion.2
  179.4 5.7 %while.55 = (s32[]{:T(128)}, f32[132,1024]{1,0:T(8,128)S(1)}, s32[]{:T(128)}, f32[15,8192]{1,0:T(8,128)S(1)}, s32[]{:T(128)}, /*index=5*/s32[]{:T(128)}, s32[]{}, s32[]{:T(128)}, s32[]{:T(128)}, s32[]{}, /*index=10*/s32[]{}) while((s32[]{:T(128)}, f32[132,1024]{1,0:T(8,128)S(1)}, s32[]{:T(128)}, f32[15,8192]{1,0:T(8,128)S(1)}, s32[]{:T(128)}, ...), condition=%wide.region_9.9_spmd, body=%wide.region_8.8_spmd.sunk | while | flops 140110336 | bytes 4180179 | solution.py:98
  180.0 0.5 convolution_add_fusion.2
  181.1 0.5 convolution_add_fusion.2
  182.3 0.5 convolution_add_fusion.2
  183.4 0.5 convolution_add_fusion.2
  184.5 0.5 convolution_add_fusion.2
  185.1 0.6 dynamic_slice.35
  186.3 1.1 dynamic-slice_bitcast_fusion.2
  187.4 9.1 %while.55 = (s32[]{:T(128)}, f32[132,1024]{1,0:T(8,128)S(1)}, s32[]{:T(128)}, f32[15,8192]{1,0:T(8,128)S(1)}, s32[]{:T(128)}, /*index=5*/s32[]{:T(128)}, s32[]{}, s32[]{:T(128)}, s32[]{:T(128)}, s32[]{}, /*index=10*/s32[]{}) while((s32[]{:T(128)}, f32[132,1024]{1,0:T(8,128)S(1)}, s32[]{:T(128)}, f32[15,8192]{1,0:T(8,128)S(1)}, s32[]{:T(128)}, ...), condition=%wide.region_9.9_spmd, body=%wide.region_8.8_spmd.sunk | while | flops 140110336 | bytes 4180179 | solution.py:98
  188.0 0.5 convolution_add_fusion.2
  189.2 0.5 convolution_add_fusion.2
  190.3 0.5 convolution_add_fusion.2
  191.4 0.5 convolution_add_fusion.2
  192.5 0.5 convolution_add_fusion.2
  193.7 0.5 convolution_add_fusion.2
  194.8 0.5 convolution_add_fusion.2
  195.9 0.5 convolution_add_fusion.2
  196.6 46.3 %collective-permute-start = (f32[12,3,1024]{2,1,0:T(4,128)S(1)}, f32[12,3,1024]{2,1,0:T(4,128)S(1)}, u32[]{:S(2)}, u32[]{:S(2)}) collective-permute-start(f32[12,3,1024]{2,1,0:T(4,128)S(1)} %slice.75), channel_id=1, source_target_pairs={{0,4},{4,8},{8,12},{1,5},{5,9},{9,13},{2,6},{6,10},{10,14},{3,7},{... | collective-permute-start | bytes 442376 | tf_op jit(solution)/shard_map/ppermute | solution.py:14
  242.9 3.5 %collective-permute-done = f32[12,3,1024]{2,1,0:T(4,128)S(1)} collective-permute-done((f32[12,3,1024]{2,1,0:T(4,128)S(1)}, f32[12,3,1024]{2,1,0:T(4,128)S(1)}, u32[]{:S(2)}, u32[]{:S(2)}) %collective-permute-start) | collective-permute-done | bytes 147488 | tf_op jit(solution)/shard_map/ppermute | solution.py:14
  246.4 0.9 scatter-add.4
  247.4 0.7 copy-done.1
  (296 shorter events, 16.3 us)
Async XLA Ops:
  6.5 23.5 %copy-start = (f32[4,16384]{1,0:T(4,128)S(1)}, f32[4,16384]{1,0:T(4,128)}, u32[]{:S(2)}) copy-start(f32[4,16384]{1,0:T(4,128)} %param.11) | copy-start | bytes 786436
  6.5 23.6 %copy-start.2 = (bf16[3,4,16384]{2,1,0:T(4,128)(2,1)S(1)}, bf16[3,4,16384]{2,1,0:T(4,128)(2,1)}, u32[]{:S(2)}) copy-start(bf16[3,4,16384]{2,1,0:T(4,128)(2,1)} %param.12) | copy-start | bytes 1179652
  6.5 20.2 %all-gather.3.cloned.1.call-start = ((), (), s32[]{:S(2)}) async-start(), calls=%async_computation.1 | async-start | bytes 1310720 | tf_op jit(solution)/shard_map/all_gather | solution.py:58
  104.4 50.5 %all-to-all-start = ((f32[4,15,8192]{2,1,0:T(8,128)}), f32[4,15,8192]{2,1,0:T(8,128)}, u32[]{:S(2)}, u32[]{:S(2)}) async-start(f32[4,15,8192]{2,1,0:T(8,128)} %bitcast.15), calls=%async_computation | async-start | bytes 4194304 | tf_op jit(solution)/shard_map/all_to_all | solution.py:85
  196.6 49.8 %collective-permute-start = (f32[12,3,1024]{2,1,0:T(4,128)S(1)}, f32[12,3,1024]{2,1,0:T(4,128)S(1)}, u32[]{:S(2)}, u32[]{:S(2)}) collective-permute-start(f32[12,3,1024]{2,1,0:T(4,128)S(1)} %slice.75), channel_id=1, source_target_pairs={{0,4},{4,8},{8,12},{1,5},{5,9},{9,13},{2,6},{6,10},{10,14},{3,7},{... | collective-permute-start | bytes 442376 | tf_op jit(solution)/shard_map/ppermute | solution.py:14
  247.3 0.7 copy-start.1
Sparse Core Ops, SparseCore 0:
  8.9 17.7 all-gather.2
where the time goes:
time: 257 us; the launch traced here: 255 us
  local copies, waits for them, and re-layouts  89.5 us (35%)
  waiting for transfers between devices  61.2 us (24%)
  starting transfers between devices  51.4 us (20%)
  other arithmetic  20.8 us (8%)
  between operations  13.6 us (5%)
  matrix products  13.4 us (5%)
  loops' own time  5.03 us (2%)
    unnamed x10, local copies, waits for them, and re-layouts  71.2 us
    ppermute x1, starting transfers between devices, shifted(): return lax.ppermute(block, axis, route)  46.3 us
    all_to_all x1, waiting for transfers between devices, local(): lax.all_to_all(buckets, 'space', split_axis=0, concat_axis=0, tiled=True)  45.4 us
    dot_general x27, matrix products, block_grad(): return jnp.dot(lifted, plane, preferred_element_type=jnp.float32)  13.4 us
    all_gather x1, waiting for transfers between devices, local(): panels = lax.all_gather(intensity, 'phase', axis=0, tiled=True)  11.7 us
    convert_element_type x27, other arithmetic, block_grad(): (along_x[:, :, None] * along_y[:, None, :]).reshape(-1, GX * GX)  6.86 us
  transfers between devices with their start and end apart: 3, of which 3 were waited for; matrix products, arithmetic and copies ran while one was open for 3% of the time, Pallas kernels for 0%

commit v1 on v0

v1 whole, which is shorter than its diff:
```python
import functools

import jax
import jax.numpy as jnp
from jax import lax
from jax.experimental import pallas as pl
from jax.experimental.pallas import tpu as pltpu
from jax.sharding import PartitionSpec as P

GX = 32
SPC = 16
GZ_DEV = 8
X_STEP = 8
MESH = pl.DeviceIdType.MESH


def spline_values(offset):
    square = offset * offset
    cube = square * offset
    remain = 1.0 - offset
    sixth = 1.0 / 6.0
    return (
        remain * remain * remain * sixth,
        (3.0 * cube - 6.0 * square + 4.0) * sixth,
        (-3.0 * cube + 3.0 * square + 3.0 * offset + 1.0) * sixth,
        cube * sixth,
    )


def spread(corner, offset, first, extent):
    width = corner.shape[1]
    row = first + lax.broadcasted_iota(jnp.int32, (extent, width), 0)
    distance = row - corner
    weights = jnp.zeros((extent, width), jnp.float32)
    for which, value in enumerate(spline_values(offset)):
        weights = jnp.where(distance == which, value, weights)
    return weights


def split_coord(coord):
    corner = coord // SPC
    return corner, (coord - corner * SPC).astype(jnp.float32) * (1.0 / SPC)


def kernel(
    n_space, n_phase, step,
    inten_ref, grad_ref, owner_ref, xy_ref, z_ref, out_ref,
    stat, heard, wx, wy, forces, lifted, acc, from_low, from_high,
    stat_send, stat_recv, up_send, up_recv, down_send, down_recv,
):
    ph_dev, samples = inten_ref.shape
    count = samples // step
    rows = 3 * ph_dev * GZ_DEV
    chunks = GX // X_STEP
    cols = X_STEP * GX
    rounds = n_phase.bit_length() - 1
    me = lax.axis_index("space")
    ph = lax.axis_index("phase")
    partners = [ph + (1 - 2 * ((ph // (1 << r)) % 2)) * (1 << r) for r in range(rounds)]

    barrier = pltpu.get_barrier_semaphore()
    for partner in partners:
        pl.semaphore_signal(barrier, inc=1, device_id={"phase": partner}, device_id_type=MESH)

    @pl.when(me > 0)
    def _():
        pl.semaphore_signal(barrier, inc=1, device_id={"space": me - 1}, device_id_type=MESH)

    @pl.when(me < n_space - 1)
    def _():
        pl.semaphore_signal(barrier, inc=1, device_id={"space": me + 1}, device_id_type=MESH)

    def ks(k):
        return pl.ds(pl.multiple_of(k * step, step), step)

    def local_stats(k, carry):
        block = inten_ref[:, ks(k)]
        mean = jnp.sum(block, axis=0, keepdims=True) * (1.0 / ph_dev)
        centered = block - mean
        stat[0, 0:1, ks(k)] = mean
        stat[0, 1:2, ks(k)] = jnp.sum(centered * centered, axis=0, keepdims=True)
        return carry

    lax.fori_loop(0, count, local_stats, 0)

    neighbours = jnp.where(me > 0, 1, 0) + jnp.where(me < n_space - 1, 1, 0)
    pl.semaphore_wait(barrier, rounds + neighbours)

    def plane_weights(k, carry):
        for axis, weights in ((0, wx), (1, wy)):
            corner, offset = split_coord(xy_ref[axis:axis + 1, ks(k)])
            weights[:, ks(k)] = spread(corner, offset, 0, GX)
        return carry

    for r in range(rounds):
        copy = pltpu.make_async_remote_copy(
            src_ref=stat.at[r],
            dst_ref=heard.at[r],
            send_sem=stat_send.at[r],
            recv_sem=stat_recv.at[r],
            device_id={"phase": partners[r]},
            device_id_type=MESH,
        )
        copy.start()
        lax.fori_loop(count * r // rounds, count * (r + 1) // rounds, plane_weights, 0)
        copy.wait()
        half = 0.5 * (ph_dev << r)

        def join(k, carry, r=r, half=half):
            apart = stat[r, 0:1, ks(k)] - heard[r, 0:1, ks(k)]
            stat[r + 1, 0:1, ks(k)] = 0.5 * (stat[r, 0:1, ks(k)] + heard[r, 0:1, ks(k)])
            stat[r + 1, 1:2, ks(k)] = (
                stat[r, 1:2, ks(k)] + heard[r, 1:2, ks(k)] + half * (apart * apart)
            )
            return carry

        lax.fori_loop(0, count, join, 0)

    def lift(k, carry):
        mean = stat[rounds, 0:1, ks(k)]
        var = stat[rounds, 1:2, ks(k)] * (1.0 / (ph_dev * n_phase))
        deviation = (inten_ref[:, ks(k)] - mean) * (2.0 * lax.rsqrt(var + 1.0))
        for c in range(3):
            forces[c * ph_dev:(c + 1) * ph_dev, :] = deviation * grad_ref[c, :, ks(k)].astype(
                jnp.float32
            )
        corner, offset = split_coord(z_ref[:, ks(k)])
        corner = corner + owner_ref[:, ks(k)] * GZ_DEV
        for o in range(n_space):
            along_z = spread(corner, offset, o * GZ_DEV, GZ_DEV)
            for pair in range(3 * ph_dev // 2):
                both = jnp.concatenate(
                    [
                        forces[2 * pair:2 * pair + 1, :] * along_z,
                        forces[2 * pair + 1:2 * pair + 2, :] * along_z,
                    ],
                    axis=0,
                )
                at = o * rows + 2 * pair * GZ_DEV
                lifted[at:at + 2 * GZ_DEV, ks(k)] = both.astype(jnp.bfloat16)
        return carry

    lax.fori_loop(0, count, lift, 0)

    def up_copy(c, j):
        return pltpu.make_async_remote_copy(
            src_ref=acc.at[c, n_space - 1 - j],
            dst_ref=from_low.at[c, j],
            send_sem=up_send.at[c, j],
            recv_sem=up_recv.at[c, j],
            device_id={"space": me + 1},
            device_id_type=MESH,
        )

    def down_copy(c, j):
        return pltpu.make_async_remote_copy(
            src_ref=acc.at[c, j],
            dst_ref=from_high.at[c, j],
            send_sem=down_send.at[c, j],
            recv_sem=down_recv.at[c, j],
            device_id={"space": me - 1},
            device_id_type=MESH,
        )

    def forward_up(c):
        def one(j, carry):
            target = n_space - 1 - j

            @pl.when((me > 0) & (me <= target))
            def _():
                up_copy(c, j).wait_recv()

            @pl.when((me > 0) & (me < target))
            def _():
                acc[c, target] += from_low[c, j]

            @pl.when(me < target)
            def _():
                up_copy(c, j).start()

            return carry

        lax.fori_loop(0, n_space - 1, one, 0)

    def forward_down(c):
        def one(j, carry):
            @pl.when((me < n_space - 1) & (me >= j))
            def _():
                down_copy(c, j).wait_recv()

            @pl.when((me < n_space - 1) & (me > j))
            def _():
                acc[c, j] += from_high[c, j]

            @pl.when(me > j)
            def _():
                down_copy(c, j).start()

            return carry

        lax.fori_loop(0, n_space - 1, one, 0)

    def slot(t, carry):
        @pl.when(t < chunks)
        def _():
            acc[t] = jnp.zeros(acc.shape[1:], jnp.float32)

            def multiply(k, inner):
                along_y = wy[:, ks(k)]
                along_x = wx[pl.ds(pl.multiple_of(t * X_STEP, X_STEP), X_STEP), ks(k)]
                plane = jnp.concatenate(
                    [(along_x[i:i + 1] * along_y).astype(jnp.bfloat16) for i in range(X_STEP)],
                    axis=0,
                )
                part = lax.dot_general(
                    lifted[:, ks(k)], plane, (((1,), (1,)), ((), ())),
                    preferred_element_type=jnp.float32,
                )
                acc[t] += part.reshape(n_space, rows, cols)
                return inner

            lax.fori_loop(0, count, multiply, 0)

        c_up = t - me
        c_down = t - (n_space - 1 - me)

        @pl.when((c_up >= 0) & (c_up < chunks))
        def _():
            forward_up(c_up)

        @pl.when((c_down >= 0) & (c_down < chunks))
        def _():
            forward_down(c_down)

        return carry

    lax.fori_loop(0, chunks + n_space - 1, slot, 0)

    for c in range(chunks):
        out_ref[:, c * cols:(c + 1) * cols] = acc[c, me]

        @pl.when(me > 0)
        def _():
            out_ref[:, c * cols:(c + 1) * cols] += from_low[c, n_space - 1 - me]

        @pl.when(me < n_space - 1)
        def _():
            out_ref[:, c * cols:(c + 1) * cols] += from_high[c, me]

    def drain(j, carry):
        for c in range(chunks):
            @pl.when(me < n_space - 1 - j)
            def _():
                up_copy(c, j).wait_send()

            @pl.when(me > j)
            def _():
                down_copy(c, j).wait_send()

        return carry

    lax.fori_loop(0, n_space - 1, drain, 0)


def local(intensity, image_grad, owner, coord_xy, coord_z):
    ph_dev, samples = intensity.shape
    n_space = lax.axis_size("space")
    n_phase = lax.axis_size("phase")
    step = min(1024, samples)
    rows = 3 * ph_dev * GZ_DEV
    chunks = GX // X_STEP
    cols = X_STEP * GX
    rounds = n_phase.bit_length() - 1
    hops = n_space - 1
    dma = pltpu.SemaphoreType.DMA
    out = pl.pallas_call(
        functools.partial(kernel, n_space, n_phase, step),
        out_shape=jax.ShapeDtypeStruct((rows, GX * GX), jnp.float32),
        in_specs=[pl.BlockSpec(memory_space=pltpu.VMEM)] * 5,
        out_specs=pl.BlockSpec(memory_space=pltpu.VMEM),
        scratch_shapes=[
            pltpu.VMEM((rounds + 1, 2, samples), jnp.float32),
            pltpu.VMEM((rounds, 2, samples), jnp.float32),
            pltpu.VMEM((GX, samples), jnp.float32),
            pltpu.VMEM((GX, samples), jnp.float32),
            pltpu.VMEM((3 * ph_dev, step), jnp.float32),
            pltpu.VMEM((n_space * rows, samples), jnp.bfloat16),
            pltpu.VMEM((chunks, n_space, rows, cols), jnp.float32),
            pltpu.VMEM((chunks, hops, rows, cols), jnp.float32),
            pltpu.VMEM((chunks, hops, rows, cols), jnp.float32),
            dma((rounds,)),
            dma((rounds,)),
            dma((chunks, hops)),
            dma((chunks, hops)),
            dma((chunks, hops)),
            dma((chunks, hops)),
        ],
        compiler_params=pltpu.CompilerParams(
            collective_id=0, has_side_effects=True, vmem_limit_bytes=58 * 1024 * 1024
        ),
    )(
        intensity,
        image_grad,
        owner.reshape(1, samples),
        coord_xy,
        coord_z.reshape(1, samples),
    )
    return out.reshape(3, ph_dev, GZ_DEV, GX * GX)


def solution(mesh):
    return jax.shard_map(
        local,
        mesh=mesh,
        in_specs=(
            P("phase", ("groups", "space")),
            P(None, "phase", ("groups", "space")),
            P(("groups", "space"), None),
            P(None, ("groups", "space")),
            P(("groups", "space")),
        ),
        out_specs=P("groups", "phase", "space", None),
        check_vma=False,
    )
```

time: 257 us -> 59.5 us (0.23)
  the two profiles are of different devices: /device:TPU:20 before, /device:TPU:0 now
where the time goes in v1:
time: 59.5 us; the launch traced here: 59.3 us
  Pallas kernels  57.6 us (97%)
  local copies, waits for them, and re-layouts  1.77 us (3%)
    pallas_call x1, Pallas kernels, local(): pl.pallas_call(functools.partial(kernel, n_space, n_phase, step), out_sha...  57.6 us
    unnamed x1, local copies, waits for them, and re-layouts  1.77 us

profile of v1, /device:TPU:0, one launch (start us, length us, event | category | flops | bytes accessed | tf_op | source)
XLA Modules:
  0.0 59.3 jit_solution(12037576895545018451)
XLA Ops:
  0.0 57.6 %shard_map.55 = f32[96,1024]{1,0:T(8,128)} custom-call(f32[4,16384]{1,0:T(4,128)} %inten_ref.1, bf16[3,4,16384]{2,1,0:T(4,128)(2,1)} %grad_ref.1, s32[1,16384]{1,0:T(1,128)} %bitcast.4, s32[2,16384]{1,0:T(2,128)} %xy_ref.1, s32[1,16384]{1,0:T(1,128)} %bitcast.5), custom_call_target="tpu_custom_call" | custom-call | tf_op jit(solution)/shard_map/pallas_call | solution.py:276
  57.6 1.8 %copy.7 = f32[3,4,8,1024]{3,2,1,0:T(8,128)} copy(f32[3,4,8,1024]{3,2,1,0:T(8,128)} %bitcast.3) | data formatting | bytes 786432

commit v2 on v1

--- a/solution.py
+++ b/solution.py
@@ -72,6 +72,11 @@
 
     def ks(k):
         return pl.ds(pl.multiple_of(k * step, step), step)
+
+    mstep = min(4096, samples)
+
+    def mk(k):
+        return pl.ds(pl.multiple_of(k * mstep, mstep), mstep)
 
     def local_stats(k, carry):
         block = inten_ref[:, ks(k)]
@@ -206,20 +211,20 @@
             acc[t] = jnp.zeros(acc.shape[1:], jnp.float32)
 
             def multiply(k, inner):
-                along_y = wy[:, ks(k)]
-                along_x = wx[pl.ds(pl.multiple_of(t * X_STEP, X_STEP), X_STEP), ks(k)]
+                along_y = wy[:, mk(k)]
+                along_x = wx[pl.ds(pl.multiple_of(t * X_STEP, X_STEP), X_STEP), mk(k)]
                 plane = jnp.concatenate(
                     [(along_x[i:i + 1] * along_y).astype(jnp.bfloat16) for i in range(X_STEP)],
                     axis=0,
                 )
                 part = lax.dot_general(
-                    lifted[:, ks(k)], plane, (((1,), (1,)), ((), ())),
+                    lifted[:, mk(k)], plane, (((1,), (1,)), ((), ())),
                     preferred_element_type=jnp.float32,
                 )
                 acc[t] += part.reshape(n_space, rows, cols)
                 return inner
 
-            lax.fori_loop(0, count, multiply, 0)
+            lax.fori_loop(0, samples // mstep, multiply, 0)
 
         c_up = t - me
         c_down = t - (n_space - 1 - me)

time: 59.5 us -> 53.9 us (0.906)
  Pallas kernels: 57.6 us -> 51.9 us
    pallas_call x1, Pallas kernels: 57.6 us -> 51.9 us  [local(): pl.pallas_call(functools.partial(kernel, n_space, n_phase, step), out_sha...]
where the time goes in v2:
time: 53.9 us; the launch traced here: 53.7 us
  Pallas kernels  51.9 us (96%)
  local copies, waits for them, and re-layouts  1.77 us (3%)
    pallas_call x1, Pallas kernels, local(): pl.pallas_call(functools.partial(kernel, n_space, n_phase, step), out_sha...  51.9 us
    unnamed x1, local copies, waits for them, and re-layouts  1.77 us

profile of v2, /device:TPU:0, one launch (start us, length us, event | category | flops | bytes accessed | tf_op | source)
XLA Modules:
  0.0 53.7 jit_solution(7131323286198197042)
XLA Ops:
  0.0 51.9 %shard_map.55 = f32[96,1024]{1,0:T(8,128)} custom-call(f32[4,16384]{1,0:T(4,128)} %inten_ref.1, bf16[3,4,16384]{2,1,0:T(4,128)(2,1)} %grad_ref.1, s32[1,16384]{1,0:T(1,128)} %bitcast.4, s32[2,16384]{1,0:T(2,128)} %xy_ref.1, s32[1,16384]{1,0:T(1,128)} %bitcast.5), custom_call_target="tpu_custom_call" | custom-call | tf_op jit(solution)/shard_map/pallas_call | solution.py:281
  51.9 1.8 %copy.7 = f32[3,4,8,1024]{3,2,1,0:T(8,128)} copy(f32[3,4,8,1024]{3,2,1,0:T(8,128)} %bitcast.3) | data formatting | bytes 786432

commit v3 on v2

--- a/solution.py
+++ b/solution.py
@@ -71,12 +71,12 @@
         pl.semaphore_signal(barrier, inc=1, device_id={"space": me + 1}, device_id_type=MESH)
 
     def ks(k):
-        return pl.ds(pl.multiple_of(k * step, step), step)
+        return pl.ds(k * step if isinstance(k, int) else pl.multiple_of(k * step, step), step)
 
     mstep = min(4096, samples)
 
     def mk(k):
-        return pl.ds(pl.multiple_of(k * mstep, mstep), mstep)
+        return pl.ds(k * mstep if isinstance(k, int) else pl.multiple_of(k * mstep, mstep), mstep)
 
     def local_stats(k, carry):
         block = inten_ref[:, ks(k)]
@@ -145,7 +145,6 @@
                 lifted[at:at + 2 * GZ_DEV, ks(k)] = both.astype(jnp.bfloat16)
         return carry
 
-    lax.fori_loop(0, count, lift, 0)
 
     def up_copy(c, j):
         return pltpu.make_async_remote_copy(
@@ -167,63 +166,80 @@
             device_id_type=MESH,
         )
 
+    top = n_space - 1
+
+    def step_up(c, j):
+        target = top - j
+
+        @pl.when((me > 0) & (me < target))
+        def _():
+            up_copy(c, j).wait_recv()
+            acc[c, target] += from_low[c, j]
+
+        @pl.when(me < target)
+        def _():
+            up_copy(c, j).start()
+
+    def step_down(c, j):
+        @pl.when((me < top) & (me > j))
+        def _():
+            down_copy(c, j).wait_recv()
+            acc[c, j] += from_high[c, j]
+
+        @pl.when(me > j)
+        def _():
+            down_copy(c, j).start()
+
     def forward_up(c):
         def one(j, carry):
-            target = n_space - 1 - j
-
-            @pl.when((me > 0) & (me <= target))
+            @pl.when(me < top - j - 1)
             def _():
-                up_copy(c, j).wait_recv()
-
-            @pl.when((me > 0) & (me < target))
-            def _():
-                acc[c, target] += from_low[c, j]
-
-            @pl.when(me < target)
-            def _():
-                up_copy(c, j).start()
+                step_up(c, j)
 
             return carry
 
-        lax.fori_loop(0, n_space - 1, one, 0)
+        lax.fori_loop(0, top - 1, one, 0)
 
     def forward_down(c):
         def one(j, carry):
-            @pl.when((me < n_space - 1) & (me >= j))
+            @pl.when(me > j + 1)
             def _():
-                down_copy(c, j).wait_recv()
-
-            @pl.when((me < n_space - 1) & (me > j))
-            def _():
-                acc[c, j] += from_high[c, j]
-
-            @pl.when(me > j)
-            def _():
-                down_copy(c, j).start()
+                step_down(c, j)
 
             return carry
 
-        lax.fori_loop(0, n_space - 1, one, 0)
+        lax.fori_loop(0, top - 1, one, 0)
+
+    def multiply_chunk(t, k):
+        along_y = wy[:, mk(k)]
+        along_x = wx[pl.ds(t * X_STEP if isinstance(t, int) else pl.multiple_of(t * X_STEP, X_STEP), X_STEP), mk(k)]
+        plane = jnp.concatenate(
+            [(along_x[i:i + 1] * along_y).astype(jnp.bfloat16) for i in range(X_STEP)],
+            axis=0,
+        )
+        part = lax.dot_general(
+            lifted[:, mk(k)], plane, (((1,), (1,)), ((), ())),
+            preferred_element_type=jnp.float32,
+        )
+        acc[t] += part.reshape(n_space, rows, cols)
+
+    acc[0] = jnp.zeros(acc.shape[1:], jnp.float32)
+    per = mstep // step
+    for k in range(samples // mstep + 1):
+        if k < samples // mstep:
+            for kk in range(k * per, (k + 1) * per):
+                lift(kk, 0)
+        if k > 0:
+            multiply_chunk(0, k - 1)
 
     def slot(t, carry):
-        @pl.when(t < chunks)
-        def _():
+        @pl.when((t > 0) & (t < chunks))
+        def _():
+            def multiply(k, inner):
+                multiply_chunk(t, k)
+                return inner
+
             acc[t] = jnp.zeros(acc.shape[1:], jnp.float32)
-
-            def multiply(k, inner):
-                along_y = wy[:, mk(k)]
-                along_x = wx[pl.ds(pl.multiple_of(t * X_STEP, X_STEP), X_STEP), mk(k)]
-                plane = jnp.concatenate(
-                    [(along_x[i:i + 1] * along_y).astype(jnp.bfloat16) for i in range(X_STEP)],
-                    axis=0,
-                )
-                part = lax.dot_general(
-                    lifted[:, mk(k)], plane, (((1,), (1,)), ((), ())),
-                    preferred_element_type=jnp.float32,
-                )
-                acc[t] += part.reshape(n_space, rows, cols)
-                return inner
-
             lax.fori_loop(0, samples // mstep, multiply, 0)
 
         c_up = t - me
@@ -241,15 +257,30 @@
 
     lax.fori_loop(0, chunks + n_space - 1, slot, 0)
 
+    def last_hop(c, carry):
+        @pl.when(me < top)
+        def _():
+            step_up(c, top - 1 - me)
+
+        @pl.when(me > 0)
+        def _():
+            step_down(c, me - 1)
+
+        return carry
+
+    lax.fori_loop(0, chunks, last_hop, 0)
+
     for c in range(chunks):
         out_ref[:, c * cols:(c + 1) * cols] = acc[c, me]
 
         @pl.when(me > 0)
         def _():
+            up_copy(c, n_space - 1 - me).wait_recv()
             out_ref[:, c * cols:(c + 1) * cols] += from_low[c, n_space - 1 - me]
 
         @pl.when(me < n_space - 1)
         def _():
+            down_copy(c, me).wait_recv()
             out_ref[:, c * cols:(c + 1) * cols] += from_high[c, me]
 
     def drain(j, carry):

time: 53.9 us -> 45.5 us (0.84)
  Pallas kernels: 51.9 us -> 43 us
    pallas_call x1, Pallas kernels: 51.9 us -> 43 us  [local(): pl.pallas_call(functools.partial(kernel, n_space, n_phase, step), out_sha...]
where the time goes in v3:
time: 45.5 us; the launch traced here: 44.7 us
  Pallas kernels  43 us (95%)
  local copies, waits for them, and re-layouts  1.77 us (4%)
    pallas_call x1, Pallas kernels, local(): pl.pallas_call(functools.partial(kernel, n_space, n_phase, step), out_sha...  43 us
    unnamed x1, local copies, waits for them, and re-layouts  1.77 us

profile of v3, /device:TPU:0, one launch (start us, length us, event | category | flops | bytes accessed | tf_op | source)
XLA Modules:
  0.0 44.7 jit_solution(7186089433697225379)
XLA Ops:
  0.0 43.0 %shard_map.55 = f32[96,1024]{1,0:T(8,128)} custom-call(f32[4,16384]{1,0:T(4,128)} %inten_ref.1, bf16[3,4,16384]{2,1,0:T(4,128)(2,1)} %grad_ref.1, s32[1,16384]{1,0:T(1,128)} %bitcast.4, s32[2,16384]{1,0:T(2,128)} %xy_ref.1, s32[1,16384]{1,0:T(1,128)} %bitcast.5), custom_call_target="tpu_custom_call" | custom-call | tf_op jit(solution)/shard_map/pallas_call | solution.py:312
  43.0 1.8 %copy.7 = f32[3,4,8,1024]{3,2,1,0:T(8,128)} copy(f32[3,4,8,1024]{3,2,1,0:T(8,128)} %bitcast.3) | data formatting | bytes 786432
